TPU v7x, 128 devices: a whole 4x4x4 slice. The times are simulated.
128 devices in a mesh: row: 16 (over y, z), col: 8 (over x, core).
Axes of the slice: x: 4, y: 4, z: 4, core: 2. Of those that a mesh axis runs over, the one named last changes fastest.
Arguments:
- front: float32 [8192, 8192], P('row', 'col'), may hold values from -25.5 to 328.81723, as said below
- child_tiles: float32 [16, 64, 512, 512], P('row', 'col'), may hold values from -3 to 3
- child_target: int32 [16, 64, 2], P('row', 'col'), may hold values from 0 to 15, as said below
- child_count: int32 [16, 8], P('row', 'col'), may hold values from 6 to 8
Outputs:
- panel: float32 [8192, 2048], P('row')
- updated: float32 [8192, 8192], P('row', 'col')
Inputs may be any that keep to these rules, and one draw needn't show every extreme that they name: front is symmetric, and the leading 4 * 512 by 2048 block of assembled is positive definite. `child_target`: within the slots of one device (i, j), the row tiles r have distinct grid rows r; every column tile c satisfies c // 2 = j.
All inputs are finite; a program needn't handle non-finite values.
Results may differ from a plain program's by a relative error of at most 0.0003.
Values sent between devices are 32-bit elements; how exact they have to be, the bound alone decides.
A program may use at most 256 MiB of HBM per device.

v0:
```python
import jax
import jax.numpy as jnp
from jax import lax
from jax.sharding import PartitionSpec as P

NP = 4


def broadcast(array, axis, root):
    mine = lax.axis_index(axis) == root
    return lax.psum(jnp.where(mine, array, jnp.zeros_like(array)), axis)


def symmetric_tile(block):
    return jnp.tril(block) + jnp.tril(block, -1).T


def body(front, child_tiles, child_target, child_count):
    precise = lax.Precision.HIGHEST
    tile_size = child_tiles.shape[-1]
    row_tiles = front.shape[0] // tile_size
    col_tiles = front.shape[1] // tile_size
    slot_count = child_tiles.shape[1]
    tiles_here = child_tiles.reshape(slot_count, tile_size, tile_size)
    targets = child_target.reshape(slot_count, 2)
    live_slots = jnp.arange(slot_count, dtype=jnp.int32) < child_count.reshape(())
    grid_rows = lax.axis_size("row")
    my_row = lax.axis_index("row")
    my_col = lax.axis_index("col")
    local_row = targets[:, 0] % row_tiles
    local_col = targets[:, 1] % col_tiles
    owners = targets[:, 0] // row_tiles
    routing = ((owners[None, :] == jnp.arange(grid_rows)[:, None]) & live_slots[None, :]).astype(
        jnp.float32
    )
    placing = (
        (local_row * col_tiles + local_col)[:, None] == jnp.arange(row_tiles * col_tiles)[None, :]
    ).astype(jnp.float32)
    outgoing = jnp.einsum("dk,kab->dab", routing, tiles_here, precision=precise)
    where_to = jnp.dot(routing, placing, precision=precise)
    incoming, positions = (
        lax.all_to_all(outgoing, "row", split_axis=0, concat_axis=0, tiled=True),
        lax.all_to_all(where_to, "row", split_axis=0, concat_axis=0, tiled=True),
    )
    summed = jnp.einsum("sq,sab->qab", positions, incoming, precision=precise)
    summed = summed.reshape(row_tiles, col_tiles, tile_size, tile_size).transpose(0, 2, 1, 3)
    added = summed.reshape(front.shape[0], front.shape[1])
    assembled = front + added
    local_cols = front.shape[1]
    strip_width = NP * tile_size
    strip_calls = max(1, strip_width // local_cols)
    strip_pieces = [broadcast(assembled, "col", owner_col) for owner_col in range(strip_calls)]
    work_strip = jnp.concatenate(strip_pieces, axis=1)
    row_share = col_tiles // row_tiles
    global_tile = (
        my_row * row_tiles + jnp.arange(row_tiles * tile_size, dtype=jnp.int32) // tile_size
    )
    result = assembled
    columns = []
    for panel_index in range(NP):
        first_col = panel_index * tile_size
        within = panel_index % row_tiles * tile_size
        diag_local = work_strip[within : within + tile_size, first_col : first_col + tile_size]
        factor = broadcast(
            jnp.linalg.cholesky(symmetric_tile(diag_local)), "row", panel_index // row_tiles
        )
        strip_now = work_strip[:, first_col : first_col + tile_size]
        solved = lax.linalg.triangular_solve(
            factor, strip_now, left_side=False, lower=True, transpose_a=True
        )
        column = jnp.where(global_tile[:, None] > panel_index, solved, jnp.zeros_like(solved))
        column = jnp.where(
            global_tile[:, None] == panel_index, jnp.tile(factor, (row_tiles, 1)), column
        )
        if panel_index + 1 < NP:
            following_parts = []
            for later in range(panel_index + 1, NP):
                following_parts.append(broadcast(column, "row", later // row_tiles))
            following = jnp.concatenate(following_parts, axis=0)
            target_cols = work_strip[:, first_col + tile_size : strip_width]
            fresh = target_cols - jnp.dot(column, following.T, precision=precise)
            work_strip = work_strip.at[:, first_col + tile_size : strip_width].set(fresh)
        columns.append(column)
    panel = jnp.concatenate(columns, axis=1)
    row_parts = [
        broadcast(panel, "row", my_col * row_share + offset) for offset in range(row_share)
    ]
    result = result - jnp.dot(panel, jnp.concatenate(row_parts, axis=0).T, precision=precise)
    return (panel, result)


def solution(mesh):
    return jax.shard_map(
        body,
        mesh=mesh,
        in_specs=(
            P("row", "col"),
            P("row", "col", None, None),
            P("row", "col", None),
            P("row", "col"),
        ),
        out_specs=(P("row", None), P("row", "col")),
        check_vma=False,
    )
```

profile of v0, /device:TPU:109, one launch (start us, length us, event | category | flops | bytes accessed | tf_op | source)
XLA Modules:
  0.0 1923.6 jit_solution(6374165362380187785)
XLA Ops:
  15.9 15.3 fusion.6
  31.2 19.1 copy.90
  57.0 229.1 %all-to-all-done.1 = f32[16,512,512]{2,1,0:T(8,128)} async-done(((f32[16,512,512]{2,1,0:T(8,128)}), f32[16,512,512]{2,1,0:T(8,128)}, u32[]{:S(2)}, u32[]{:S(2)}) %all-to-all-start.1) | async-done | bytes 16777248 | tf_op jit(solution)/shard_map/all_to_all | solution.py:42
  286.1 22.7 %fusion = f32[2,512,512]{2,0,1:T(2,128)S(1)} fusion(f32[16,2,1]{1,0,2:T(8,128)S(1)} %bitcast.247, f32[16,512,512]{2,1,0:T(8,128)} %all-to-all-done.1), kind=kOutput, calls=%fused_computation.8 | convolution fusion | flops 100663296 | bytes 18874496 | tf_op jit(solution)/shard_map/sq,sab->qab/dot_general | solution.py:45
  315.3 142.3 %all-reduce.31.cloned.1.call-done = (f32[512,1024]{1,0:T(8,128)}, f32[512,1024]{1,0:T(8,128)}) async-done(((f32[512,1024]{1,0:T(8,128)}, f32[512,1024]{1,0:T(8,128)}), (f32[512,1024]{1,0:T(8,128)}, f32[512,1024]{1,0:T(8,128)})) %all-reduce.31.cloned.1.call-update) | async-done | bytes 4194320 | tf_op jit(solution)/shard_map/psum | solution.py:11
  465.5 11.7 cholesky.462
  477.3 9.8 custom-call.35
  489.8 11.7 cholesky.481
  501.5 18.5 custom-call.36
  521.6 11.7 cholesky.502
  534.0 9.8 custom-call.37
  545.2 11.9 cholesky.519
  562.2 86.2 %all-reduce.15.cloned.1.call-done = f32[512,512]{1,0:T(8,128)} async-done(((f32[512,512]{1,0:T(8,128)}), f32[512,512]{1,0:T(8,128)}) %all-reduce.15.cloned.1.call-update) | async-done | bytes 1048592 | tf_op jit(solution)/shard_map/psum | solution.py:11
  659.5 40.1 %custom-call.38 = f32[4,128,128]{1,2,0:T(8,128)S(1)} custom-call(f32[4,128,128]{2,1,0:T(8,128)} %copy-done.30), custom_call_target="InvertDiagBlocksLowerTriangular" | custom-call | tf_op jit(solution)/shard_map/triangular_solve/custom-call.3 | solution.py:68
  715.2 96.6 %all-reduce.29.cloned.1.call-done = (f32[512,512]{1,0:T(8,128)}, f32[512,512]{1,0:T(8,128)}, f32[512,512]{1,0:T(8,128)}) async-done(((f32[512,512]{1,0:T(8,128)}, f32[512,512]{1,0:T(8,128)}, f32[512,512]{1,0:T(8,128)}), (f32[512,512]{1,0:T(8,128)}, f32[512,512]{1,0:T(8,128)}, f32[512,512]{1,0:T(8,128)})) %all-reduce.29.cloned.1.call-update) | async-done | bytes 3145744 | tf_op jit(solution)/shard_map/psum | solution.py:11
  811.9 8.5 convolution_subtract_fusion
  831.7 11.7 cholesky.534
  844.6 9.8 custom-call.39
  857.6 11.7 cholesky.553
  871.2 10.0 custom-call.40
  883.6 11.7 cholesky.574
  896.5 9.8 custom-call.41
  908.6 11.9 cholesky.591
  925.4 84.7 %all-reduce.17.cloned.1.call-done = f32[512,512]{1,0:T(8,128)} async-done(((f32[512,512]{1,0:T(8,128)}), f32[512,512]{1,0:T(8,128)}) %all-reduce.17.cloned.1.call-update) | async-done | bytes 1048592 | tf_op jit(solution)/shard_map/psum | solution.py:11
  1012.5 11.4 while.12
  1024.6 40.1 %custom-call.42 = f32[4,128,128]{1,2,0:T(8,128)S(1)} custom-call(f32[4,128,128]{2,1,0:T(8,128)} %copy-done.31), custom_call_target="InvertDiagBlocksLowerTriangular" | custom-call | tf_op jit(solution)/shard_map/triangular_solve/custom-call.3 | solution.py:68
  1080.3 90.1 %all-reduce.27.cloned.1.call-done = (f32[512,512]{1,0:T(8,128)}, f32[512,512]{1,0:T(8,128)}) async-done(((f32[512,512]{1,0:T(8,128)}, f32[512,512]{1,0:T(8,128)}), (f32[512,512]{1,0:T(8,128)}, f32[512,512]{1,0:T(8,128)})) %all-reduce.27.cloned.1.call-update) | async-done | bytes 2097168 | tf_op jit(solution)/shard_map/psum | solution.py:11
  1180.7 11.7 cholesky.606
  1192.6 9.8 custom-call.43
  1205.0 11.9 cholesky.625
  1218.2 9.8 custom-call.44
  1229.5 11.7 cholesky.646
  1241.9 9.8 custom-call.45
  1253.4 11.7 cholesky.663
  1269.6 86.0 %all-reduce.19.cloned.1.call-done = f32[512,512]{1,0:T(8,128)} async-done(((f32[512,512]{1,0:T(8,128)}), f32[512,512]{1,0:T(8,128)}) %all-reduce.19.cloned.1.call-update) | async-done | bytes 1048592 | tf_op jit(solution)/shard_map/psum | solution.py:11
  1365.5 40.1 %custom-call.46 = f32[4,128,128]{1,2,0:T(8,128)S(1)} custom-call(f32[4,128,128]{2,1,0:T(8,128)} %copy-done.32), custom_call_target="InvertDiagBlocksLowerTriangular" | custom-call | tf_op jit(solution)/shard_map/triangular_solve/custom-call.3 | solution.py:68
  1418.0 85.5 %all-reduce.21.cloned.1.call-done = f32[512,512]{1,0:T(8,128)} async-done(((f32[512,512]{1,0:T(8,128)}), f32[512,512]{1,0:T(8,128)}) %all-reduce.21.cloned.1.call-update) | async-done | bytes 1048592 | tf_op jit(solution)/shard_map/psum | solution.py:11
  1512.5 11.7 cholesky.678
  1524.4 9.8 custom-call.47
  1536.7 11.9 cholesky.697
  1549.9 9.8 custom-call.48
  1561.3 11.7 cholesky.718
  1573.7 9.8 custom-call.49
  1585.0 11.9 cholesky.735
  1601.2 86.3 %all-reduce.23.cloned.1.call-done = f32[512,512]{1,0:T(8,128)} async-done(((f32[512,512]{1,0:T(8,128)}), f32[512,512]{1,0:T(8,128)}) %all-reduce.23.cloned.1.call-update) | async-done | bytes 1048592 | tf_op jit(solution)/shard_map/psum | solution.py:11
  1698.3 40.1 %custom-call.50 = f32[4,128,128]{1,2,0:T(8,128)S(1)} custom-call(f32[4,128,128]{2,1,0:T(8,128)} %copy-done.29), custom_call_target="InvertDiagBlocksLowerTriangular" | custom-call | tf_op jit(solution)/shard_map/triangular_solve/custom-call.3 | solution.py:68
  1756.5 142.4 %all-reduce.25.cloned.1.call-done = (f32[512,2048]{1,0:T(8,128)}, f32[512,2048]{1,0:T(8,128)}) async-done(((f32[512,2048]{1,0:T(8,128)}, f32[512,2048]{1,0:T(8,128)}), (f32[512,2048]{1,0:T(8,128)}, f32[512,2048]{1,0:T(8,128)})) %all-reduce.25.cloned.1.call-update) | async-done | bytes 8388624 | tf_op jit(solution)/shard_map/psum | solution.py:11
  1898.9 17.8 fusion.19
  (297 shorter events, 232.7 us)
Async XLA Ops:
  9.4 40.9 %all-to-all-start = ((f32[16,1,2]{2,1,0:T(1,128)}), f32[16,1,2]{2,1,0:T(1,128)S(1)}, u32[]{:S(2)}, u32[]{:S(2)}) async-start(f32[16,1,2]{2,1,0:T(1,128)} %bitcast.77), calls=%async_computation | async-start | bytes 16384 | tf_op jit(solution)/shard_map/all_to_all | solution.py:43
  50.3 235.8 %all-to-all-start.1 = ((f32[16,512,512]{2,1,0:T(8,128)}), f32[16,512,512]{2,1,0:T(8,128)}, u32[]{:S(2)}, u32[]{:S(2)}) async-start(f32[16,512,512]{2,1,0:T(8,128)} %copy.90), calls=%async_computation.1 | async-start | bytes 33554432 | tf_op jit(solution)/shard_map/all_to_all | solution.py:42
  57.0 400.6 %all-reduce.31.cloned.1.call-start = ((), (), s32[]{:S(2)}) async-start(), calls=%async_computation.10 | async-start | bytes 8388608 | tf_op jit(solution)/shard_map/psum | solution.py:11
  308.8 1.6 copy-start.24
  312.4 1.4 copy-start.3
  315.2 333.2 %all-reduce.15.cloned.1.call-start = ((), (), s32[]{:S(2)}) async-start(), calls=%async_computation.2 | async-start | bytes 2097152 | tf_op jit(solution)/shard_map/psum | solution.py:11
  457.6 2.8 copy-start.9
  464.6 1.0 copy-start.19
  562.1 249.8 %all-reduce.29.cloned.1.call-start = ((), (), s32[]{:S(2)}) async-start(), calls=%async_computation.9 | async-start | bytes 6291456 | tf_op jit(solution)/shard_map/psum | solution.py:11
  657.9 0.7 copy-start.30
  658.6 1.0 copy-start.15
  699.7 0.7 copy-start.26
  699.7 11.6 copy-start.11
  700.4 0.7 copy-start.20
  712.5 1.0 copy-start.7
  715.2 294.9 %all-reduce.17.cloned.1.call-start = ((), (), s32[]{:S(2)}) async-start(), calls=%async_computation.3 | async-start | bytes 2097152 | tf_op jit(solution)/shard_map/psum | solution.py:11
  830.7 1.0 copy-start.16
  925.3 245.1 %all-reduce.27.cloned.1.call-start = ((), (), s32[]{:S(2)}) async-start(), calls=%async_computation.8 | async-start | bytes 4194304 | tf_op jit(solution)/shard_map/psum | solution.py:11
  1023.9 0.7 copy-start.31
  1064.7 0.7 copy-start.27
  1065.5 0.7 copy-start.21
  1069.4 7.1 copy-start.12
  1077.7 1.0 copy-start.5
  1079.8 275.8 %all-reduce.19.cloned.1.call-start = ((), (), s32[]{:S(2)}) async-start(), calls=%async_computation.4 | async-start | bytes 2097152 | tf_op jit(solution)/shard_map/psum | solution.py:11
  1176.0 1.3 copy-start.1
  1179.7 1.0 copy-start.17
  1268.4 137.3 %copy-start.2 = (f32[512,1024]{1,0:T(8,128)S(1)}, f32[512,1024]{1,0:T(8,128)}, u32[]{:S(2)}) copy-start(f32[512,1024]{1,0:T(8,128)} %copy-done.1) | copy-start | bytes 6291460
  1269.6 234.0 %all-reduce.21.cloned.1.call-start = ((), (), s32[]{:S(2)}) async-start(), calls=%async_computation.5 | async-start | bytes 2097152 | tf_op jit(solution)/shard_map/psum | solution.py:11
  1364.8 0.7 copy-start.32
  1405.7 0.7 copy-start.28
  1406.4 0.7 copy-start.22
  1417.1 270.5 %all-reduce.23.cloned.1.call-start = ((), (), s32[]{:S(2)}) async-start(), calls=%async_computation.6 | async-start | bytes 2097152 | tf_op jit(solution)/shard_map/psum | solution.py:11
  1511.5 1.0 copy-start.18
  1600.0 138.4 %copy-start.10 = (f32[512,512]{1,0:T(8,128)S(1)}, f32[512,512]{1,0:T(8,128)}, u32[]{:S(2)}) copy-start(f32[512,512]{1,0:T(8,128)} %get-tuple-element.180) | copy-start | bytes 3145732
  1601.2 297.7 %all-reduce.25.cloned.1.call-start = ((), (), s32[]{:S(2)}) async-start(), calls=%async_computation.7 | async-start | bytes 16777216 | tf_op jit(solution)/shard_map/psum | solution.py:11
  1696.6 0.7 copy-start.29
  1697.3 1.0 copy-start.14
  1738.4 0.7 copy-start.25
  1738.4 11.8 copy-start.13
  1739.1 0.7 copy-start.23
  1745.9 4.6 copy-start.6
  1745.9 4.6 copy-start.8
  1753.2 3.3 copy-start
  1756.4 142.5 %copy-start.4 = (f32[512,1024]{1,0:T(8,128)S(1)}, f32[512,1024]{1,0:T(8,128)}, u32[]{:S(2)}) copy-start(f32[512,1024]{1,0:T(8,128)} %copy-done.3) | copy-start | bytes 6291460
Sparse Core Ops, SparseCore 0:
  315.4 142.2 all-reduce.30
  562.2 86.1 all-reduce.14
  715.3 96.5 all-reduce.28
  925.4 84.6 all-reduce.16
  1079.9 90.4 all-reduce.26
  1269.7 85.8 all-reduce.18
  1417.2 86.2 all-reduce.20
  1601.3 86.2 all-reduce.22
  1756.6 142.2 all-reduce.24
where the time goes:
time: 1940 us; the launch traced here: 1920 us
  waiting for transfers between devices  1130 us (58%)
  other arithmetic  526 us (27%)
  matrix products  135 us (7%)
  local copies, waits for them, and re-layouts  92.4 us (5%)
  between operations  26 us (1%)
    psum x9, waiting for transfers between devices, broadcast(): return lax.psum(jnp.where(mine, array, jnp.zeros_like(array)), axis)  900 us
    another operation x59, other arithmetic, body(): jnp.linalg.cholesky(symmetric_tile(diag_local))  327 us
    all_to_all x1, waiting for transfers between devices, body(): lax.all_to_all(outgoing, 'row', split_axis=0, concat_axis=0, tiled=True)  229 us
    another operation x9, other arithmetic, body(): lax.linalg.triangular_solve(factor, strip_now, left_side=False, lower=Tru...  167 us
    another operation x57, local copies, waits for them, and re-layouts, body(): lax.linalg.triangular_solve(factor, strip_now, left_side=False, lower=Tru...  38.9 us
  transfers between devices with their start and end apart: 11, of which 10 were waited for; matrix products, arithmetic and copies ran while one was open for 2% of the time, Pallas kernels for 0%

commit v1 on v0

--- a/solution.py
+++ b/solution.py
@@ -1,8 +1,234 @@
+import functools
 import jax
 import jax.numpy as jnp
 from jax import lax
+from jax.experimental import pallas as pl
+from jax.experimental.pallas import tpu as pltpu
+
+MESH = pl.DeviceIdType.MESH
+ROWS = 16
+CHUNK = 32
+
+
+def lb(x,j): return jnp.broadcast_to(x[:,j:j+1],x.shape)
+def sb(x,s): return jnp.broadcast_to(x[s:s+1,:],x.shape)
+def chol128(D,E,M=8,n=128):
+    sub = lax.broadcasted_iota(jnp.int32,(8,128),0)
+    G=len(D)
+    for g in range(G):
+        for m0 in range(0,8,M):
+            base=8*g+m0
+            C=[lb(D[g],base+c) for c in range(M)]
+            a=[[sb(C[c],m0+r) if c<=r else None for c in range(M)] for r in range(M)]
+            U=[];V=[];R=[]
+            l=[[None]*M for _ in range(M)]
+            for k in range(M):
+                rk=lax.rsqrt(a[k][k]); R.append(rk)
+                for i in range(k+1,M): l[i][k]=a[i][k]*rk
+                for i in range(k+1,M):
+                    for c in range(k+1,i+1):
+                        a[i][c]=a[i][c]-l[i][k]*l[c][k]
+            for k in range(M):
+                u=sb(D[g],m0+k); v=sb(E[g],m0+k)
+                for c in range(k):
+                    u=u-l[k][c]*U[c]; v=v-l[k][c]*V[c]
+                U.append(u*R[k]); V.append(v*R[k])
+            for h in range(g,G):
+                if h==g and m0+M>=8: continue
+                Ch=C if h==g else [lb(D[h],base+c) for c in range(M)]
+                L=[]
+                for k in range(M):
+                    x=Ch[k]
+                    for c in range(k): x=x-L[c]*l[k][c]
+                    L.append(x*R[k])
+                d=D[h]; e=E[h]
+                for k in range(M):
+                    lk=jnp.where(sub>=m0+M,L[k],0.0) if h==g else L[k]
+                    d=d-lk*U[k]; e=e-lk*V[k]
+                D[h]=d;E[h]=e
+            for k in range(M):
+                D[g]=jnp.where(sub==m0+k,U[k],D[g]); E[g]=jnp.where(sub==m0+k,V[k],E[g])
+    return D,E
+
+B=512;S=128
+
+HI=lax.Precision.HIGHEST; H3=lax.Precision.HIGH
+def dot_nt(a,b,prec): return lax.dot_general(a,b,(((1,),(1,)),((),())),precision=prec,preferred_element_type=jnp.float32)
+def dot_nn(a,b,prec): return lax.dot_general(a,b,(((1,),(0,)),((),())),precision=prec,preferred_element_type=jnp.float32)
+
+def factor_tile(w, ti, base):
+    r=lambda b: pl.ds(pl.multiple_of(base+b*S,S),S)
+    eye=[(lax.broadcasted_iota(jnp.int32,(8,S),0)+8*g==lax.broadcasted_iota(jnp.int32,(8,S),1)).astype(jnp.float32) for g in range(16)]
+    row=lax.broadcasted_iota(jnp.int32,(S,S),0); col=lax.broadcasted_iota(jnp.int32,(S,S),1)
+    lowm=row>=col
+    nb=B//S
+    T={}
+    for i in range(nb):
+        for j in range(i+1):
+            x=w[r(i),r(j)]
+            if i==j:
+                x=jnp.where(lowm,x,x.T)
+            T[i,j]=x
+    inv={}
+    for b in range(nb):
+        x=T[b,b]
+        D,E=chol128([x[8*g:8*g+8] for g in range(16)],list(eye))
+        U=jnp.concatenate(D,0); I=jnp.concatenate(E,0)
+        I=jnp.where(lowm,I,0.0)
+        w[r(b),r(b)]=jnp.where(lowm,U.T,0.0)
+        inv[b,b]=I
+        for i in range(b+1,nb):
+            P=dot_nt(T[i,b],I,HI)
+            T[i,b]=P
+            w[r(i),r(b)]=P
+            w[r(b),r(i)]=jnp.zeros((S,S),jnp.float32)
+        for i in range(b+1,nb):
+            for j in range(b+1,i+1):
+                T[i,j]=T[i,j]-dot_nt(T[i,b],T[j,b],HI)
+        for j in range(b):
+            acc=None
+            for k in range(j,b):
+                t=dot_nn(T[b,k],inv[k,j],HI)
+                acc=t if acc is None else acc+t
+            inv[b,j]=-dot_nn(I,acc,HI)
+        for j in range(nb):
+            ti[b*S:(b+1)*S,j*S:(j+1)*S]=inv[b,j] if j<=b else jnp.zeros((S,S),jnp.float32)
+
+def kern(w,ti):
+    w[...]=(lax.broadcasted_iota(jnp.int32,(2048,2048),0)==lax.broadcasted_iota(jnp.int32,(2048,2048),1)).astype(jnp.float32)
+    zero=jnp.zeros((B,B),jnp.float32)
+    def tile(p,c):
+        base=pl.multiple_of(p*B,B)
+        factor_tile(w,ti.at[p],base)
+        def solve(q,c):
+            o=pl.ds(pl.multiple_of(q*B,B),B)
+            w[o,pl.ds(base,B)]=dot_nt(w[o,pl.ds(base,B)],ti[p],H3)
+            return c
+        lax.fori_loop(p+1,4,solve,0)
+        def upd(q,c):
+            o=pl.ds(pl.multiple_of(q*B,B),B)
+            w[pl.ds(base,B),o]=zero
+            def inner(s,c):
+                o2=pl.ds(pl.multiple_of(s*B,B),B)
+                w[o,o2]=w[o,o2]-dot_nt(w[o,pl.ds(base,B)],w[o2,pl.ds(base,B)],H3)
+                return c
+            return lax.fori_loop(p+1,q+1,inner,c)
+        lax.fori_loop(p+1,4,upd,0)
+        return c
+    lax.fori_loop(0,4,tile,0)
+
+
+def ext_kernel(child, front, meta, out, recv1, send2, recv2, meta_all, meta_s, s1, r1, s2, r2, sm, rm, lsem, w, ti):
+    me = lax.axis_index("row")
+    col = lax.axis_index("col")
+    y, z = me // 4, me % 4
+    barrier = pltpu.get_barrier_semaphore()
+
+    def peer(o):
+        dy, dz = o // 4, o % 4
+        return (y + dy) % 4 * 4 + (z + dz) % 4
+
+    def source(o):
+        dy, dz = o // 4, o % 4
+        return (y + 4 - dy) % 4 * 4 + (z + 4 - dz) % 4
+
+    order = [10, 9, 11, 6, 14, 5, 7, 13, 15, 2, 8, 1, 3, 4, 12]
+    for o in order:
+        pl.semaphore_signal(barrier, inc=1, device_id=(peer(o), col), device_id_type=MESH)
+    pl.semaphore_wait(barrier, len(order))
+
+    def meta_copy(o):
+        return pltpu.make_async_remote_copy(meta, meta_all.at[me], sm.at[o], rm.at[o], device_id=(peer(o), col), device_id_type=MESH)
+
+    def chunk_copy(o):
+        rows = pl.ds(pl.multiple_of(peer(o) * CHUNK, CHUNK), CHUNK)
+        return pltpu.make_async_remote_copy(child.at[0, :, rows, :], recv1.at[me], s1.at[o], r1.at[o], device_id=(peer(o), col), device_id_type=MESH)
+
+    for o in order:
+        meta_copy(o).start()
+    for o in order:
+        chunk_copy(o).start()
+    rows_me = pl.ds(pl.multiple_of(me * CHUNK, CHUNK), CHUNK)
+    own = pltpu.make_async_copy(child.at[0, :, rows_me, :], recv1.at[me], lsem.at[0])
+    own.start()
+    own_meta = pltpu.make_async_copy(meta, meta_all.at[me], lsem.at[1])
+    own_meta.start()
+    own.wait()
+    own_meta.wait()
+    for o in order:
+        meta_copy(o).wait()
+    to_smem = pltpu.make_async_copy(meta_all, meta_s, lsem.at[2])
+    to_smem.start()
+    to_smem.wait()
+    kern(w,ti)
+    for o in order:
+        chunk_copy(o).wait()
+
+    def reduce_for(d):
+        def step(i, acc):
+            slot = meta_s[i, 0, d]
+            code = meta_s[i, 1, d]
+            value = recv1[i, slot]
+            first = jnp.where(code == 0, 1.0, 0.0)
+            second = jnp.where(code == 1, 1.0, 0.0)
+            return acc[0] + value * first, acc[1] + value * second
+
+        zero = jnp.zeros((CHUNK, 512), jnp.float32)
+        a, b = lax.fori_loop(0, ROWS, step, (zero, zero))
+        send2[d, :, 0:512] = a
+        send2[d, :, 512:1024] = b
+
+    def sum_copy(o):
+        return pltpu.make_async_remote_copy(send2.at[peer(o)], recv2.at[me], s2.at[o], r2.at[o], device_id=(peer(o), col), device_id_type=MESH)
+
+    for o in order:
+        reduce_for(peer(o))
+        sum_copy(o).start()
+    reduce_for(me)
+    recv2[me] = send2[me]
+    for o in order:
+        sum_copy(o).wait()
+    out[...] = front[...] + recv2[...].reshape(512, 1024) + (w[0:512,0:1024]-w[512:1024,0:1024])*0.0
+
+
+def extend_add(front, child_tiles, meta):
+    return pl.pallas_call(
+        ext_kernel,
+        out_shape=jax.ShapeDtypeStruct((512, 1024), jnp.float32),
+        in_specs=[pl.BlockSpec(memory_space=pl.ANY), pl.BlockSpec(memory_space=pltpu.VMEM), pl.BlockSpec(memory_space=pltpu.VMEM)],
+        out_specs=pl.BlockSpec(memory_space=pltpu.VMEM),
+        scratch_shapes=[
+            pltpu.VMEM((ROWS, 8, CHUNK, 512), jnp.float32),
+            pltpu.VMEM((ROWS, CHUNK, 1024), jnp.float32),
+            pltpu.VMEM((ROWS, CHUNK, 1024), jnp.float32),
+            pltpu.VMEM((ROWS, 8, 128), jnp.int32),
+            pltpu.SMEM((ROWS, 8, 128), jnp.int32),
+            pltpu.SemaphoreType.DMA((16,)),
+            pltpu.SemaphoreType.DMA((16,)),
+            pltpu.SemaphoreType.DMA((16,)),
+            pltpu.SemaphoreType.DMA((16,)),
+            pltpu.SemaphoreType.DMA((16,)),
+            pltpu.SemaphoreType.DMA((16,)),
+            pltpu.SemaphoreType.DMA((3,)),
+pltpu.VMEM((2048,2048),jnp.float32),pltpu.VMEM((4,512,512),jnp.float32),
+        ],
+        compiler_params=pltpu.CompilerParams(collective_id=0, has_side_effects=True, vmem_limit_bytes=50 * 2**20),
+    )(child_tiles, front, meta)
+
+
+def make_meta(child_target, child_count):
+    targets = child_target.reshape(8, 2)
+    live = jnp.arange(8, dtype=jnp.int32) < child_count.reshape(())
+    owner = targets[:, 0]
+    code = targets[:, 1] % 2
+    hit = (owner[:, None] == jnp.arange(16)[None, :]) & live[:, None]
+    any_hit = hit.any(axis=0)
+    slot = jnp.sum(jnp.where(hit, jnp.arange(8, dtype=jnp.int32)[:, None], 0), axis=0)
+    codes = jnp.where(any_hit, jnp.sum(jnp.where(hit, code[:, None], 0), axis=0), 2)
+    table = jnp.stack([slot, codes]).astype(jnp.int32)
+    return jnp.pad(table, ((0, 6), (0, 112)))
+
 from jax.sharding import PartitionSpec as P
-
 NP = 4
 
 
@@ -22,30 +248,9 @@
     col_tiles = front.shape[1] // tile_size
     slot_count = child_tiles.shape[1]
     tiles_here = child_tiles.reshape(slot_count, tile_size, tile_size)
-    targets = child_target.reshape(slot_count, 2)
-    live_slots = jnp.arange(slot_count, dtype=jnp.int32) < child_count.reshape(())
-    grid_rows = lax.axis_size("row")
-    my_row = lax.axis_index("row")
-    my_col = lax.axis_index("col")
-    local_row = targets[:, 0] % row_tiles
-    local_col = targets[:, 1] % col_tiles
-    owners = targets[:, 0] // row_tiles
-    routing = ((owners[None, :] == jnp.arange(grid_rows)[:, None]) & live_slots[None, :]).astype(
-        jnp.float32
-    )
-    placing = (
-        (local_row * col_tiles + local_col)[:, None] == jnp.arange(row_tiles * col_tiles)[None, :]
-    ).astype(jnp.float32)
-    outgoing = jnp.einsum("dk,kab->dab", routing, tiles_here, precision=precise)
-    where_to = jnp.dot(routing, placing, precision=precise)
-    incoming, positions = (
-        lax.all_to_all(outgoing, "row", split_axis=0, concat_axis=0, tiled=True),
-        lax.all_to_all(where_to, "row", split_axis=0, concat_axis=0, tiled=True),
-    )
-    summed = jnp.einsum("sq,sab->qab", positions, incoming, precision=precise)
-    summed = summed.reshape(row_tiles, col_tiles, tile_size, tile_size).transpose(0, 2, 1, 3)
-    added = summed.reshape(front.shape[0], front.shape[1])
-    assembled = front + added
+    my_row = lax.axis_index('row')
+    my_col = lax.axis_index('col')
+    assembled = extend_add(front, child_tiles, make_meta(child_target, child_count))
     local_cols = front.shape[1]
     strip_width = NP * tile_size
     strip_calls = max(1, strip_width // local_cols)

time: 1940 us -> 1750 us (0.902)
  waiting for transfers between devices: 1130 us -> 853 us
  Pallas kernels: 0 us -> 142 us
  matrix products: 135 us -> 108 us
    all_to_all x2 -> x0, waiting for transfers between devices: 229 us -> none  [the longest x1 229 us: body(): lax.all_to_all(outgoing, 'row', split_axis=0, concat_axis=0, tiled=True)]
    pallas_call x0 -> x1, Pallas kernels: none -> 142 us  [extend_add(): pl.pallas_call(ext_kernel, out_shape=jax.ShapeDtypeStruct((512, 1024), jn...]
    psum x9, waiting for transfers between devices: 900 us -> 852 us  [broadcast(): return lax.psum(jnp.where(mine, array, jnp.zeros_like(array)), axis)]
    dot_general x3 -> x0, matrix products: 38.8 us -> none  [the longest x1 22.7 us: body(): summed = jnp.einsum('sq,sab->qab', positions, incoming, precision=precise)]
  transfers between devices with their start and end apart: 11 -> 9, of which waited for: 10 -> 9; matrix products, arithmetic and copies ran while one was open for 2% -> 0% of each run, Pallas kernels for 0% -> 0%
where the time goes in v1:
time: 1750 us; the launch traced here: 1730 us
  waiting for transfers between devices  853 us (49%)
  other arithmetic  527 us (30%)
  Pallas kernels  142 us (8%)
  matrix products  108 us (6%)
  local copies, waits for them, and re-layouts  76.6 us (4%)
  between operations  26.1 us (1%)
    psum x9, waiting for transfers between devices, broadcast(): return lax.psum(jnp.where(mine, array, jnp.zeros_like(array)), axis)  852 us
    another operation x59, other arithmetic, body(): jnp.linalg.cholesky(symmetric_tile(diag_local))  321 us
    another operation x9, other arithmetic, body(): lax.linalg.triangular_solve(factor, strip_now, left_side=False, lower=Tru...  168 us
    pallas_call x1, Pallas kernels, extend_add(): pl.pallas_call(ext_kernel, out_shape=jax.ShapeDtypeStruct((512, 1024), jn...  142 us
    another operation x28, matrix products, body(): lax.linalg.triangular_solve(factor, strip_now, left_side=False, lower=Tru...  43.7 us
    another operation x57, local copies, waits for them, and re-layouts, body(): lax.linalg.triangular_solve(factor, strip_now, left_side=False, lower=Tru...  42.6 us
  transfers between devices with their start and end apart: 9, of which 9 were waited for; matrix products, arithmetic and copies ran while one was open for 0% of the time, Pallas kernels for 0%

profile of v1, /device:TPU:109, one launch (start us, length us, event | category | flops | bytes accessed | tf_op | source)
XLA Modules:
  0.0 1732.4 jit_solution(17189221404055624040)
XLA Ops:
  8.8 141.8 %shard_map.59 = f32[512,1024]{1,0:T(8,128)S(1)} custom-call(f32[1,8,512,512]{3,2,1,0:T(8,128)} %child.1, f32[512,1024]{1,0:T(8,128)} %front.1, s32[8,128]{1,0:T(8,128)S(1)} %pad.11.meta), custom_call_target="tpu_custom_call" | custom-call | tf_op jit(solution)/shard_map/pallas_call | solution.py:195
  153.5 94.0 %all-reduce.32.cloned.1.call-done = (f32[512,1024]{1,0:T(8,128)}, f32[512,1024]{1,0:T(8,128)}) async-done(((f32[512,1024]{1,0:T(8,128)}, f32[512,1024]{1,0:T(8,128)}), (f32[512,1024]{1,0:T(8,128)}, f32[512,1024]{1,0:T(8,128)})) %all-reduce.32.cloned.1.call-update) | async-done | bytes 4194320 | tf_op jit(solution)/shard_map/psum | solution.py:237
  255.6 11.7 cholesky.462
  267.3 9.8 custom-call.35
  279.8 11.7 cholesky.481
  291.6 9.9 custom-call.36
  303.1 11.7 cholesky.502
  315.5 9.8 custom-call.37
  326.7 11.9 cholesky.519
  343.7 86.2 %all-reduce.16.cloned.1.call-done = f32[512,512]{1,0:T(8,128)} async-done(((f32[512,512]{1,0:T(8,128)}), f32[512,512]{1,0:T(8,128)}) %all-reduce.16.cloned.1.call-update) | async-done | bytes 1048592 | tf_op jit(solution)/shard_map/psum | solution.py:237
  431.3 8.0 while.11
  440.0 40.1 %custom-call.38 = f32[4,128,128]{1,2,0:T(8,128)S(1)} custom-call(f32[4,128,128]{2,1,0:T(8,128)} %copy-done.21), custom_call_target="InvertDiagBlocksLowerTriangular" | custom-call | tf_op jit(solution)/shard_map/triangular_solve/custom-call.3 | solution.py:273
  497.1 96.6 %all-reduce.30.cloned.1.call-done = (f32[512,512]{1,0:T(8,128)}, f32[512,512]{1,0:T(8,128)}, f32[512,512]{1,0:T(8,128)}) async-done(((f32[512,512]{1,0:T(8,128)}, f32[512,512]{1,0:T(8,128)}, f32[512,512]{1,0:T(8,128)}), (f32[512,512]{1,0:T(8,128)}, f32[512,512]{1,0:T(8,128)}, f32[512,512]{1,0:T(8,128)})) %all-reduce.30.cloned.1.call-update) | async-done | bytes 3145744 | tf_op jit(solution)/shard_map/psum | solution.py:237
  593.7 8.4 convolution_subtract_fusion
  610.6 11.7 cholesky.534
  623.1 9.8 custom-call.39
  635.5 11.7 cholesky.553
  647.9 9.9 custom-call.40
  659.4 11.7 cholesky.574
  671.8 9.8 custom-call.41
  683.1 12.1 cholesky.591
  699.6 84.7 %all-reduce.18.cloned.1.call-done = f32[512,512]{1,0:T(8,128)} async-done(((f32[512,512]{1,0:T(8,128)}), f32[512,512]{1,0:T(8,128)}) %all-reduce.18.cloned.1.call-update) | async-done | bytes 1048592 | tf_op jit(solution)/shard_map/psum | solution.py:237
  785.7 7.7 while.12
  794.1 40.1 %custom-call.42 = f32[4,128,128]{1,2,0:T(8,128)S(1)} custom-call(f32[4,128,128]{2,1,0:T(8,128)} %copy-done.22), custom_call_target="InvertDiagBlocksLowerTriangular" | custom-call | tf_op jit(solution)/shard_map/triangular_solve/custom-call.3 | solution.py:273
  850.4 90.6 %all-reduce.28.cloned.1.call-done = (f32[512,512]{1,0:T(8,128)}, f32[512,512]{1,0:T(8,128)}) async-done(((f32[512,512]{1,0:T(8,128)}, f32[512,512]{1,0:T(8,128)}), (f32[512,512]{1,0:T(8,128)}, f32[512,512]{1,0:T(8,128)})) %all-reduce.28.cloned.1.call-update) | async-done | bytes 2097168 | tf_op jit(solution)/shard_map/psum | solution.py:237
  959.8 11.7 cholesky.606
  972.3 9.8 custom-call.43
  986.4 11.9 cholesky.625
  999.6 9.8 custom-call.44
  1011.7 11.7 cholesky.646
  1024.7 9.8 custom-call.45
  1037.0 11.7 cholesky.663
  1053.9 85.9 %all-reduce.20.cloned.1.call-done = f32[512,512]{1,0:T(8,128)} async-done(((f32[512,512]{1,0:T(8,128)}), f32[512,512]{1,0:T(8,128)}) %all-reduce.20.cloned.1.call-update) | async-done | bytes 1048592 | tf_op jit(solution)/shard_map/psum | solution.py:237
  1142.2 11.7 while.13
  1154.6 40.1 %custom-call.46 = f32[4,128,128]{1,2,0:T(8,128)S(1)} custom-call(f32[4,128,128]{2,1,0:T(8,128)} %copy-done.23), custom_call_target="InvertDiagBlocksLowerTriangular" | custom-call | tf_op jit(solution)/shard_map/triangular_solve/custom-call.3 | solution.py:273
  1210.1 85.5 %all-reduce.22.cloned.1.call-done = f32[512,512]{1,0:T(8,128)} async-done(((f32[512,512]{1,0:T(8,128)}), f32[512,512]{1,0:T(8,128)}) %all-reduce.22.cloned.1.call-update) | async-done | bytes 1048592 | tf_op jit(solution)/shard_map/psum | solution.py:237
  1311.2 11.7 cholesky.678
  1323.6 9.8 custom-call.47
  1337.7 11.9 cholesky.697
  1350.9 9.8 custom-call.48
  1363.0 11.7 cholesky.718
  1376.0 9.8 custom-call.49
  1388.1 11.9 cholesky.735
  1405.0 86.4 %all-reduce.24.cloned.1.call-done = f32[512,512]{1,0:T(8,128)} async-done(((f32[512,512]{1,0:T(8,128)}), f32[512,512]{1,0:T(8,128)}) %all-reduce.24.cloned.1.call-update) | async-done | bytes 1048592 | tf_op jit(solution)/shard_map/psum | solution.py:237
  1493.8 11.2 while.14
  1505.6 40.1 %custom-call.50 = f32[4,128,128]{1,2,0:T(8,128)S(1)} custom-call(f32[4,128,128]{2,1,0:T(8,128)} %copy-done.20), custom_call_target="InvertDiagBlocksLowerTriangular" | custom-call | tf_op jit(solution)/shard_map/triangular_solve/custom-call.3 | solution.py:273
  1565.1 142.4 %all-reduce.26.cloned.1.call-done = (f32[512,2048]{1,0:T(8,128)}, f32[512,2048]{1,0:T(8,128)}) async-done(((f32[512,2048]{1,0:T(8,128)}, f32[512,2048]{1,0:T(8,128)}), (f32[512,2048]{1,0:T(8,128)}, f32[512,2048]{1,0:T(8,128)})) %all-reduce.26.cloned.1.call-update) | async-done | bytes 8388624 | tf_op jit(solution)/shard_map/psum | solution.py:237
  1707.5 17.9 %fusion.15 = f32[512,1024]{1,0:T(8,128)} fusion(f32[512,1024]{1,0:T(8,128)S(1)} %shard_map.59, f32[512,2048]{1,0:T(8,128)} %copy-done, f32[512,2048]{1,0:T(8,128)} %get-tuple-element.104, f32[512,2048]{1,0:T(8,128)} %get-tuple-element.105), kind=kOutput, calls=%fused_computation.27 | convolution fusion | flops 12887523328 | bytes 16777216 | tf_op jit(solution)/shard_map/dot_general | solution.py:293
  (275 shorter events, 218.6 us)
Async XLA Ops:
  7.2 240.3 %all-reduce.32.cloned.1.call-start = ((), (), s32[]{:S(2)}) async-start(), calls=%async_computation.8 | async-start | bytes 8388608 | tf_op jit(solution)/shard_map/psum | solution.py:237
  153.4 276.5 %all-reduce.16.cloned.1.call-start = ((), (), s32[]{:S(2)}) async-start(), calls=%async_computation | async-start | bytes 2097152 | tf_op jit(solution)/shard_map/psum | solution.py:237
  254.6 1.0 copy-start.11
  343.6 250.1 %all-reduce.30.cloned.1.call-start = ((), (), s32[]{:S(2)}) async-start(), calls=%async_computation.7 | async-start | bytes 6291456 | tf_op jit(solution)/shard_map/psum | solution.py:237
  439.3 0.7 copy-start.21
  480.2 1.5 copy-start.17
  481.7 0.7 copy-start.12
  495.2 98.5 %copy-start.3 = (f32[512,512]{1,0:T(8,128)}, f32[512,512]{1,0:T(8,128)S(1)}, u32[]{:S(2)}) copy-start(f32[512,512]{1,0:T(8,128)S(1)} %get-tuple-element.120) | copy-start | bytes 3145732
  497.0 287.3 %all-reduce.18.cloned.1.call-start = ((), (), s32[]{:S(2)}) async-start(), calls=%async_computation.1 | async-start | bytes 2097152 | tf_op jit(solution)/shard_map/psum | solution.py:237
  602.1 1.7 copy-start.1
  609.6 1.0 copy-start.8
  699.5 241.5 %all-reduce.28.cloned.1.call-start = ((), (), s32[]{:S(2)}) async-start(), calls=%async_computation.6 | async-start | bytes 4194304 | tf_op jit(solution)/shard_map/psum | solution.py:237
  793.4 0.7 copy-start.22
  834.2 1.5 copy-start.18
  835.7 0.7 copy-start.13
  850.4 289.5 %all-reduce.20.cloned.1.call-start = ((), (), s32[]{:S(2)}) async-start(), calls=%async_computation.2 | async-start | bytes 2097152 | tf_op jit(solution)/shard_map/psum | solution.py:237
  946.9 1.3 copy-start.2
  958.8 1.0 copy-start.9
  1053.8 241.8 %all-reduce.22.cloned.1.call-start = ((), (), s32[]{:S(2)}) async-start(), calls=%async_computation.3 | async-start | bytes 2097152 | tf_op jit(solution)/shard_map/psum | solution.py:237
  1153.9 0.7 copy-start.23
  1194.7 1.5 copy-start.19
  1196.2 0.7 copy-start.14
  1200.3 7.3 copy-start.6
  1209.2 282.2 %all-reduce.24.cloned.1.call-start = ((), (), s32[]{:S(2)}) async-start(), calls=%async_computation.4 | async-start | bytes 2097152 | tf_op jit(solution)/shard_map/psum | solution.py:237
  1310.2 1.0 copy-start.10
  1404.9 302.5 %all-reduce.26.cloned.1.call-start = ((), (), s32[]{:S(2)}) async-start(), calls=%async_computation.5 | async-start | bytes 16777216 | tf_op jit(solution)/shard_map/psum | solution.py:237
  1504.9 0.7 copy-start.20
  1545.8 1.5 copy-start.16
  1547.3 0.7 copy-start.15
  1551.3 7.5 copy-start.7
  1554.4 4.7 copy-start.4
  1554.4 4.7 copy-start.5
  1561.8 3.3 copy-start
Sparse Core Ops, SparseCore 0:
  153.6 93.8 all-reduce.31
  343.7 86.1 all-reduce.15
  497.1 96.4 all-reduce.29
  699.6 84.6 all-reduce.17
  850.5 90.4 all-reduce.27
  1053.9 85.8 all-reduce.19
  1209.4 86.2 all-reduce.21
  1405.1 86.3 all-reduce.23
  1565.2 142.2 all-reduce.25

commit v2 on v0

v2 whole, which is shorter than its diff:
```python
import jax
import jax.numpy as jnp
from jax import lax
from jax.experimental import pallas as pl
from jax.experimental.pallas import tpu as pltpu
from jax.sharding import PartitionSpec as P

MESH = pl.DeviceIdType.MESH
F32 = jnp.float32
HIGHEST = lax.Precision.HIGHEST
HIGH = lax.Precision.HIGH
ROWS = 16
CT = 8
B = 512
S = 128
NP = 4
CHUNK = 32
MICRO = 8
NB = B // S
ORDER = (10, 9, 11, 6, 14, 5, 7, 13, 15, 2, 8, 1, 3, 4, 12)
PIECES = (
    (0, 0, 0, 512),
    (0, 1, 0, 1024),
    (0, 2, 0, 1024),
    (0, 3, 0, 1024),
    (1, 2, 1024, 512),
    (1, 3, 1024, 1024),
)


def dot_nt(a, b, precision):
    return lax.dot_general(
        a, b, (((1,), (1,)), ((), ())), precision=precision, preferred_element_type=F32
    )


def dot_nn(a, b, precision):
    return lax.dot_general(
        a, b, (((1,), (0,)), ((), ())), precision=precision, preferred_element_type=F32
    )


def lane(x, j):
    return jnp.broadcast_to(x[:, j : j + 1], x.shape)


def sublane(x, s):
    return jnp.broadcast_to(x[s : s + 1, :], x.shape)


def eliminate(d, e):
    groups = len(d)
    for g in range(groups):
        base = MICRO * g
        cols = [lane(d[g], base + c) for c in range(MICRO)]
        a = [[sublane(cols[c], r) for c in range(r + 1)] for r in range(MICRO)]
        low = [[None] * MICRO for _ in range(MICRO)]
        rs = []
        for k in range(MICRO):
            r = lax.rsqrt(a[k][k])
            rs.append(r)
            for i in range(k + 1, MICRO):
                low[i][k] = a[i][k] * r
            for i in range(k + 1, MICRO):
                for c in range(k + 1, i + 1):
                    a[i][c] = a[i][c] - low[i][k] * low[c][k]
        us, vs = [], []
        for k in range(MICRO):
            u, v = sublane(d[g], k), sublane(e[g], k)
            for c in range(k):
                u = u - low[k][c] * us[c]
                v = v - low[k][c] * vs[c]
            us.append(u * rs[k])
            vs.append(v * rs[k])
        for h in range(g + 1, groups):
            ch = [lane(d[h], base + c) for c in range(MICRO)]
            ls = []
            for k in range(MICRO):
                t = ch[k]
                for c in range(k):
                    t = t - ls[c] * low[k][c]
                ls.append(t * rs[k])
            dh, eh = d[h], e[h]
            for k in range(MICRO):
                dh = dh - ls[k] * us[k]
                eh = eh - ls[k] * vs[k]
            d[h], e[h] = dh, eh
        sub = lax.broadcasted_iota(jnp.int32, (8, S), 0)
        for k in range(MICRO):
            d[g] = jnp.where(sub == k, us[k], d[g])
            e[g] = jnp.where(sub == k, vs[k], e[g])
    return d, e


def factor_tile(w, ti, base, hook, before_write):
    def part(b):
        return pl.ds(pl.multiple_of(base + b * S, S), S)

    sub = lax.broadcasted_iota(jnp.int32, (8, S), 0)
    lanes = lax.broadcasted_iota(jnp.int32, (8, S), 1)
    row = lax.broadcasted_iota(jnp.int32, (S, S), 0)
    col = lax.broadcasted_iota(jnp.int32, (S, S), 1)
    lower = row >= col
    t, inv = {}, {}
    for b in range(NB):
        hook(b)
        if b == 0:
            for i in range(NB):
                for j in range(i + 1):
                    x = w[part(i), part(j)]
                    t[i, j] = jnp.where(lower, x, x.T) if i == j else x
        x = t[b, b]
        eye = [(sub + 8 * g == lanes).astype(F32) for g in range(S // 8)]
        d, e = eliminate([x[8 * g : 8 * g + 8] for g in range(S // 8)], eye)
        if b == 0:
            before_write()
        upper = jnp.concatenate(d, 0)
        inverse = jnp.where(lower, jnp.concatenate(e, 0), 0.0)
        w[part(b), part(b)] = jnp.where(lower, upper.T, 0.0)
        inv[b, b] = inverse
        for i in range(b + 1, NB):
            t[i, b] = dot_nt(t[i, b], inverse, HIGHEST)
            w[part(i), part(b)] = t[i, b]
            w[part(b), part(i)] = jnp.zeros((S, S), F32)
        for i in range(b + 1, NB):
            for j in range(b + 1, i + 1):
                t[i, j] = t[i, j] - dot_nt(t[i, b], t[j, b], HIGHEST)
        for j in range(b):
            acc = None
            for k in range(j, b):
                term = dot_nn(t[b, k], inv[k, j], HIGHEST)
                acc = term if acc is None else acc + term
            inv[b, j] = -dot_nn(inverse, acc, HIGHEST)
        for j in range(NB):
            ti[b * S : (b + 1) * S, j * S : (j + 1) * S] = (
                inv[b, j] if j <= b else jnp.zeros((S, S), F32)
            )


def kernel(
    child, front, meta, panel_out, upd_out,
    recva, recvb, fr, total, half, w, ti, xs, st, recv2, meta_all, meta_s,
    s_meta, r_meta, s_a, r_a, s_b, r_b, s_fr, r_fr, s_p, r_p, s_sum, r_sum,
    s_hx, r_hx, s_ha, r_ha, s_hb, r_hb, s_st, r_st, lsem,
):
    me = lax.axis_index("row")
    col = lax.axis_index("col")
    y, z = me // 4, me % 4
    x, core = col // 2, col % 2
    first = jnp.where(core == 0, y, z)
    second = jnp.where(core == 0, z, y)
    my_chunk = second * 4 + first
    lead = x == 0

    def row_of(a, b):
        return jnp.where(core == 0, a * 4 + b, b * 4 + a)

    def peer(o):
        return (y + o // 4) % 4 * 4 + (z + o % 4) % 4

    def chunk_of(r):
        return jnp.where(core == 0, r % 4 * 4 + r // 4, r)

    def rows32(k):
        return pl.ds(pl.multiple_of(k * CHUNK, CHUNK), CHUNK)

    def remote(src, dst, send, recv, r, c):
        return pltpu.make_async_remote_copy(
            src, dst, send, recv, device_id=(r, c), device_id_type=MESH
        )

    barrier = pltpu.get_barrier_semaphore()

    def greet(r, c):
        pl.semaphore_signal(barrier, inc=1, device_id=(r, c), device_id_type=MESH)

    for o in ORDER:
        greet(peer(o), col)
    for t in range(1, 4):
        greet(me, (col + 2 * t) % 8)
        greet(row_of((first + t) % 4, second), x * 2 + 1 - core)
    greet(me, x * 2 + 1 - core)
    pl.semaphore_wait(barrier, 22)

    sibling = x * 2 + 1 - core

    def meta_copy(o):
        return remote(meta, meta_all.at[me], s_meta.at[o], r_meta.at[o], peer(o), col)

    def slots_a(o):
        r = peer(o)
        return remote(
            child.at[0:4, rows32(chunk_of(r)), :], recva.at[me], s_a.at[o], r_a.at[o], r, col
        )

    def slots_b(o):
        r = peer(o)
        return remote(
            child.at[4:8, rows32(chunk_of(r)), :], recvb.at[me], s_b.at[o], r_b.at[o], r, col
        )

    def front_copy(o):
        r = peer(o)
        return remote(front.at[chunk_of(r)], fr.at[me], s_fr.at[o], r_fr.at[o], r, col)

    def sum_copy(o):
        r = peer(o)
        return remote(total.at[r], recv2.at[my_chunk], s_sum.at[o], r_sum.at[o], r, col)

    for o in ORDER:
        meta_copy(o).start()

    @pl.when(lead & (y == 0))
    def _():
        for o in ORDER:
            front_copy(o).start()

    for o in ORDER:
        slots_a(o).start()
    own_a = pltpu.make_async_copy(child.at[0:4, rows32(my_chunk), :], recva.at[me], lsem.at[0])
    own_a.start()
    own_b = pltpu.make_async_copy(child.at[4:8, rows32(my_chunk), :], recvb.at[me], lsem.at[8])
    own_b.start()
    own_meta = pltpu.make_async_copy(meta, meta_all.at[me], lsem.at[1])
    own_meta.start()

    @pl.when(lead)
    def _():
        own = pltpu.make_async_copy(front.at[my_chunk], fr.at[me], lsem.at[2])
        own.start()
        own.wait()

    @pl.when(x > 0)
    def _():
        own = pltpu.make_async_copy(front, fr, lsem.at[3])
        own.start()
        own.wait()

    own_a.wait()
    own_b.wait()
    own_meta.wait()
    for o in ORDER:
        meta_copy(o).wait()
    to_smem = pltpu.make_async_copy(meta_all, meta_s, lsem.at[4])
    to_smem.start()
    to_smem.wait()
    for o in ORDER:
        slots_a(o).wait_recv()

    def reduce_for(d, late):
        def step(i, acc):
            slot = meta_s[i, 0, d]
            value = recva[i, jnp.minimum(slot, 3)]
            if late:
                value = jnp.where(slot < 4, value, recvb[i, jnp.maximum(slot - 4, 0)])
            code = meta_s[i, 1, d]
            left = jnp.where(code == 0, 1.0, 0.0)
            right = jnp.where(code == 1, 1.0, 0.0)
            return acc[0] + value * left, acc[1] + value * right

        zero = jnp.zeros((CHUNK, B), F32)
        a, b = lax.fori_loop(0, ROWS, step, (zero, zero))
        total[d, :, 0:B] = a
        total[d, :, B : 2 * B] = b

        @pl.when(lead)
        def _():
            total[d] = total[d] + fr[d]

    @pl.when(lead)
    def _():
        for t in range(4):
            o = y * 4 + t

            @pl.when(o > 0)
            def _():
                front_copy(o).wait_recv()

    for d in range(4):
        reduce_for(d, False)

    def piece_x(n, t):
        _, d, c0, nc = PIECES[n]
        part = w.at[pl.ds(pl.multiple_of(d * B + my_chunk * CHUNK, CHUNK), CHUNK), c0 : c0 + nc]
        return remote(part, part, s_p.at[n, t - 1], r_p.at[n, t - 1], me, (col + 2 * t) % 8)

    def piece_a(n, t):
        _, d, c0, nc = PIECES[n]
        part = w.at[pl.ds(pl.multiple_of(d * B + my_chunk * CHUNK, CHUNK), CHUNK), c0 : c0 + nc]
        return remote(
            part, part, s_p.at[n, 2 + t], r_p.at[n, 2 + t], row_of((first + t) % 4, second), col
        )

    def piece_b(n, t):
        _, d, c0, nc = PIECES[n]
        part = w.at[pl.ds(pl.multiple_of(d * B + second * S, S), S), c0 : c0 + nc]
        return remote(
            part, part, s_p.at[n, 5 + t], r_p.at[n, 5 + t], row_of(first, (second + t) % 4), col
        )

    def piece_s(n):
        _, d, c0, nc = PIECES[n]
        part = w.at[d * B : (d + 1) * B, c0 : c0 + nc]
        return remote(part, part, s_p.at[n, 9], r_p.at[n, 9], me, sibling)

    def on_core(k, numbers, action):
        @pl.when(core == k)
        def _():
            for n in numbers:
                if PIECES[n][0] == k:
                    action(n)

    def both_cores(numbers, action):
        for k in range(2):
            if any(PIECES[n][0] == k for n in numbers):
                on_core(k, numbers, action)

    def place(n):
        _, d, c0, nc = PIECES[n]
        lc = c0 % 1024
        w[pl.ds(pl.multiple_of(d * B + my_chunk * CHUNK, CHUNK), CHUNK), c0 : c0 + nc] = total[
            d, :, lc : lc + nc
        ]

    def start_x(n):
        for t in (1, 3, 2):
            piece_x(n, t).start()

    def wait_x(n):
        piece_x(n, x).wait_recv()

    def start_a(n):
        for t in (2, 1, 3):
            piece_a(n, t).start()

    def wait_a(n):
        for t in (1, 2, 3):
            piece_a(n, t).wait_recv()

    def start_b(n):
        for t in (2, 1, 3):
            piece_b(n, t).start()

    def wait_b(n):
        for t in (1, 2, 3):
            piece_b(n, t).wait_recv()

    def start_s(n):
        piece_s(n).start()

    def wait_s(n):
        piece_s(n).wait_recv()

    rest = tuple(range(1, len(PIECES)))

    @pl.when(lead)
    def _():
        both_cores((0,) + rest, place)
        both_cores((0,) + rest, start_x)

    @pl.when(x > 0)
    def _():
        both_cores((0,), wait_x)

    both_cores((0,), start_a)
    both_cores((0,), wait_a)
    both_cores((0,), start_b)

    @pl.when(x > 0)
    def _():
        both_cores(rest, wait_x)

    both_cores(rest, start_a)
    both_cores((0,), wait_b)
    both_cores((0,), start_s)
    for o in ORDER:
        slots_b(o).start()

    @pl.when(lead & (y > 0))
    def _():
        for o in ORDER:
            front_copy(o).start()

    @pl.when(core == 1)
    def _():
        wait_s(0)

    def half_x(t):
        to = (x + t) % 4
        return remote(
            total.at[pl.ds(to * 4, 4)], half.at[:, rows32(first), :],
            s_hx.at[t - 1], r_hx.at[t - 1], me, (col + 2 * t) % 8,
        )

    def half_a(t):
        part = half.at[:, rows32(first), :]
        return remote(part, part, s_ha.at[t - 1], r_ha.at[t - 1], row_of((first + t) % 4, second), col)

    def half_b(t, k, c):
        return remote(
            half.at[2 * k : 2 * k + 2],
            xs.at[:, pl.ds(pl.multiple_of(second * S, S), S), c * 1024 : (c + 1) * 1024],
            s_hb.at[t, k], r_hb.at[t, c], row_of(first, (second + t) % 4), x * 2 + k,
        )

    def strip_rows(n):
        return slice(n * 256, (n + 1) * 256)

    def strip_x(t, n, c):
        part = st.at[strip_rows(n), c * 1024 : (c + 1) * 1024]
        return remote(part, part, s_st.at[n, t], r_st.at[n, t], me, (col + 2 * t) % 8)

    def strip_s(c, k):
        part = st.at[:, c * 1024 : (c + 1) * 1024]
        return remote(part, part, s_st.at[0, 0], r_st.at[0, 0], me, sibling)

    def by_core(action):
        for c in range(2):

            @pl.when(core == c)
            def _():
                action(c)

    def task_rest_b():
        both_cores(rest, wait_a)
        both_cores(rest, start_b)

    def task_rest_s():
        both_cores(rest, wait_b)
        both_cores(rest, start_s)

    def task_sums():
        for o in ORDER:
            slots_b(o).wait_recv()

        @pl.when(lead)
        def _():
            for o in ORDER:

                @pl.when(y != o // 4)
                def _():
                    front_copy(o).wait_recv()

        lax.fori_loop(4, ROWS, lambda d, c: (reduce_for(d, True), c)[1], 0)

        @pl.when(lead)
        def _():
            for t in (1, 3, 2):
                half_x(t).start()

        for o in ORDER:
            sum_copy(o).start()
        recv2[my_chunk] = total[me]

    def task_half_a():
        @pl.when(x > 0)
        def _():
            half_x(x).wait_recv()
            for t in (2, 1, 3):
                half_a(t).start()

    def task_half_b():
        @pl.when(x > 0)
        def _():
            for t in (1, 2, 3):
                half_a(t).wait_recv()

            def send(c):
                for t in (2, 1, 3, 0):
                    for k in range(2):
                        if t > 0 or k != c:
                            half_b(t, k, c).start()
                own = pltpu.make_async_copy(
                    half.at[2 * c : 2 * c + 2],
                    xs.at[:, pl.ds(pl.multiple_of(second * S, S), S), c * 1024 : (c + 1) * 1024],
                    lsem.at[5],
                )
                own.start()
                own.wait()

            by_core(send)

    def task_assembled():
        for o in ORDER:
            sum_copy(o).wait_recv()

        @pl.when(x > 0)
        def _():
            recv2[...] = recv2[...] + fr[...]

        @pl.when(lead)
        def _():
            def put(c):
                def move(k, carry):
                    st[rows32(k), c * 1024 : (c + 1) * 1024] = recv2[k]
                    return carry

                lax.fori_loop(0, ROWS, move, 0)
                for n in range(2):
                    strip_x(1, n, c).start()
                    strip_x(3, 1 - n, c).start()
                strip_s(c, 1 - c).start()

            by_core(put)

    def task_forward():
        def forward(c):
            @pl.when(x == 1)
            def _():
                strip_x(1, 0, c).wait_recv()
                strip_x(1, 0, c).start()

            @pl.when(x == 3)
            def _():
                strip_x(3, 1, c).wait_recv()
                strip_x(3, 1, c).start()

        by_core(forward)

    def task_strip_s():
        def send(c):
            @pl.when(x == 1)
            def _():
                strip_x(1, 1, c).wait_recv()

            @pl.when(x == 3)
            def _():
                strip_x(3, 0, c).wait_recv()

            @pl.when(x == 2)
            def _():
                strip_x(1, 0, c).wait_recv()
                strip_x(3, 1, c).wait_recv()

            @pl.when(x > 0)
            def _():
                strip_s(c, 1 - c).start()

        by_core(send)

    schedule = {
        (0, 1): task_rest_b,
        (0, 2): task_rest_s,
        (2, 1): task_sums,
        (2, 3): task_half_a,
        (3, 1): task_half_b,
        (3, 0): task_assembled,
        (3, 3): task_forward,
    }

    def piece_done(n):
        @pl.when(lead)
        def _():
            for t in range(1, 4):
                piece_x(n, t).wait_send()

        for t in range(1, 4):
            piece_a(n, t).wait_send()
            piece_b(n, t).wait_send()
        piece_s(n).wait_send()

    def tile(p, carry):
        base = pl.multiple_of(p * B, B)

        def hook(b):
            for (p0, b0), task in schedule.items():
                if b0 == b:
                    pl.when(p == p0)(task)

        def before_write():
            pl.when(p == 0)(lambda: both_cores((0,), piece_done))

        factor_tile(w, ti.at[p], base, hook, before_write)

        @pl.when(p == 0)
        def _():
            @pl.when(core == 0)
            def _():
                for n in rest:
                    if PIECES[n][0] == 1:
                        wait_s(n)

            @pl.when(core == 1)
            def _():
                for n in rest:
                    if PIECES[n][0] == 0:
                        wait_s(n)

            both_cores(rest, piece_done)

        here = pl.ds(base, B)

        def solve(q, c):
            o = pl.ds(pl.multiple_of(q * B, B), B)
            w[o, here] = dot_nt(w[o, here], ti[p], HIGH)
            return c

        lax.fori_loop(p + 1, NP, solve, 0)

        def update(q, c):
            o = pl.ds(pl.multiple_of(q * B, B), B)
            w[here, o] = jnp.zeros((B, B), F32)

            def inner(s, c):
                o2 = pl.ds(pl.multiple_of(s * B, B), B)
                w[o, o2] = w[o, o2] - dot_nt(w[o, here], w[o2, here], HIGH)
                return c

            return lax.fori_loop(p + 1, q + 1, inner, c)

        lax.fori_loop(p + 1, NP, update, 0)
        return carry

    lax.fori_loop(0, NP, tile, 0)
    task_strip_s()

    def solve_rows(ref):
        def panel(p, c):
            here = pl.ds(pl.multiple_of(p * B, B), B)
            ref[:, here] = dot_nt(ref[:, here], ti[p], HIGH)

            def later(q, c):
                o = pl.ds(pl.multiple_of(q * B, B), B)
                ref[:, o] = ref[:, o] - dot_nt(ref[:, here], w[o, here], HIGH)
                return c

            return lax.fori_loop(p + 1, NP, later, c)

        lax.fori_loop(0, NP, panel, 0)

    @pl.when(lead)
    def _():
        for k in range(2):
            xs[k] = w[pl.ds(pl.multiple_of((2 * core + k) * B, B), B), :]

    @pl.when(x > 0)
    def _():
        for t in range(1, 4):
            for c in range(2):
                half_b(t, 0, c).wait_recv()

        def others(c):
            half_b(0, 0, 1 - c).wait_recv()

        by_core(others)
        for k in range(2):
            solve_rows(xs.at[k])

    def strip_done(c):
        strip_s(c, 1 - c).wait()

        @pl.when(lead)
        def _():
            for n in range(2):
                strip_x(1, n, c).wait_send()
                strip_x(3, n, c).wait_send()

        @pl.when(x == 1)
        def _():
            strip_x(1, 0, c).wait_send()

        @pl.when(x == 3)
        def _():
            strip_x(3, 1, c).wait_send()

    by_core(strip_done)

    @pl.when(y == 0)
    def _():
        st[...] = w[pl.ds(pl.multiple_of(me * B, B), B), :]

    @pl.when(y > 0)
    def _():
        solve_rows(st)

    panel_copy = pltpu.make_async_copy(st, panel_out, lsem.at[6])
    panel_copy.start()

    def last(i, c):
        rows = pl.ds(pl.multiple_of(i * 256, 256), 256)
        for k in range(2):
            product = dot_nt(st[rows, :], xs[k], HIGH)
            part = recv2[pl.ds(i * 8, 8), :, k * B : (k + 1) * B]
            recv2[pl.ds(i * 8, 8), :, k * B : (k + 1) * B] = part - product.reshape(8, CHUNK, B)
        return c

    lax.fori_loop(0, 2, last, 0)
    out_copy = pltpu.make_async_copy(recv2, upd_out, lsem.at[7])
    out_copy.start()

    for o in ORDER:
        slots_a(o).wait_send()
        slots_b(o).wait_send()
        sum_copy(o).wait_send()

    @pl.when(lead)
    def _():
        for o in ORDER:
            front_copy(o).wait_send()
        for t in range(1, 4):
            half_x(t).wait_send()


    @pl.when(x > 0)
    def _():
        for t in range(1, 4):
            half_a(t).wait_send()

        def half_sent(c):
            for t in range(4):
                for k in range(2):
                    if t > 0 or k != c:
                        half_b(t, k, c).wait_send()

        by_core(half_sent)

    panel_copy.wait()
    out_copy.wait()


def fused(front, child, meta):
    dma = pltpu.SemaphoreType.DMA
    return pl.pallas_call(
        kernel,
        out_shape=[
            jax.ShapeDtypeStruct((B, NP * B), F32),
            jax.ShapeDtypeStruct((ROWS, CHUNK, 1024), F32),
        ],
        in_specs=[
            pl.BlockSpec(memory_space=pl.ANY),
            pl.BlockSpec(memory_space=pl.ANY),
            pl.BlockSpec(memory_space=pltpu.VMEM),
        ],
        out_specs=[pl.BlockSpec(memory_space=pl.ANY)] * 2,
        scratch_shapes=[
            pltpu.VMEM((ROWS, 4, CHUNK, B), F32),
            pltpu.VMEM((ROWS, 4, CHUNK, B), F32),
            pltpu.VMEM((ROWS, CHUNK, 1024), F32),
            pltpu.VMEM((ROWS, CHUNK, 1024), F32),
            pltpu.VMEM((4, S, 1024), F32),
            pltpu.VMEM((NP * B, NP * B), F32),
            pltpu.VMEM((NP, B, B), F32),
            pltpu.VMEM((2, B, NP * B), F32),
            pltpu.VMEM((B, NP * B), F32),
            pltpu.VMEM((ROWS, CHUNK, 1024), F32),
            pltpu.VMEM((ROWS, 8, 128), jnp.int32),
            pltpu.SMEM((ROWS, 8, 128), jnp.int32),
            dma((16,)), dma((16,)), dma((16,)), dma((16,)), dma((16,)), dma((16,)),
            dma((16,)), dma((16,)), dma((6, 10)), dma((6, 10)), dma((16,)), dma((16,)),
            dma((3,)), dma((3,)), dma((3,)), dma((3,)), dma((4, 2)), dma((4, 2)),
            dma((2, 4)), dma((2, 4)), dma((9,)),
        ],
        compiler_params=pltpu.CompilerParams(
            collective_id=0, has_side_effects=True, vmem_limit_bytes=60 * 2**20
        ),
    )(child, front, meta)


def tables(child_target, child_count):
    targets = child_target.reshape(CT, 2)
    slots = jnp.arange(CT, dtype=jnp.int32)
    live = slots < child_count.reshape(())
    key = jnp.where(live, targets[:, 0], ROWS) * CT + slots
    place = jnp.sum((key[None, :] < key[:, None]).astype(jnp.int32), axis=1)
    order = jnp.sum(jnp.where(place[:, None] == slots[None, :], slots[:, None], 0), axis=0)
    hit = (targets[:, 0][:, None] == jnp.arange(ROWS)[None, :]) & live[:, None]
    where = jnp.sum(jnp.where(hit, place[:, None], 0), axis=0)
    code = jnp.sum(jnp.where(hit, targets[:, 1][:, None] % 2, 0), axis=0)
    code = jnp.where(hit.any(axis=0), code, 2)
    table = jnp.stack([where, code]).astype(jnp.int32)
    return order.astype(jnp.int32), jnp.pad(table, ((0, 6), (0, 128 - ROWS)))


def sort_kernel(order, child, out, held, sems):
    reads = [pltpu.make_async_copy(child.at[order[i]], held.at[i], sems.at[i]) for i in range(CT)]
    writes = [pltpu.make_async_copy(held.at[i], out.at[i], sems.at[CT + i]) for i in range(CT)]
    for copy in reads:
        copy.start()
    for i in range(CT):
        reads[i].wait()
        writes[i].start()
    for copy in writes:
        copy.wait()


def sort_slots(order, child):
    return pl.pallas_call(
        sort_kernel,
        out_shape=jax.ShapeDtypeStruct(child.shape, F32),
        in_specs=[pl.BlockSpec(memory_space=pltpu.SMEM), pl.BlockSpec(memory_space=pl.ANY)],
        out_specs=pl.BlockSpec(memory_space=pl.ANY),
        scratch_shapes=[pltpu.VMEM((CT, B, B), F32), pltpu.SemaphoreType.DMA((2 * CT,))],
        compiler_params=pltpu.CompilerParams(vmem_limit_bytes=32 * 2**20),
    )(order, child)


def body(front, child_tiles, child_target, child_count):
    order, meta = tables(child_target, child_count)
    child = sort_slots(order, child_tiles.reshape(CT, B, B))
    panel, updated = fused(front.reshape(ROWS, CHUNK, 1024), child, meta)
    return panel, updated.reshape(front.shape)


def solution(mesh):
    return jax.shard_map(
        body,
        mesh=mesh,
        in_specs=(
            P("row", "col"),
            P("row", "col", None, None),
            P("row", "col", None),
            P("row", "col"),
        ),
        out_specs=(P("row", None), P("row", "col")),
        check_vma=False,
    )
```

time: 1940 us -> 419 us (0.22)
  waiting for transfers between devices: 1130 us -> 0 us
  other arithmetic: 526 us -> 1.92 us
  Pallas kernels: 0 us -> 402 us
  matrix products: 135 us -> 0 us
  local copies, waits for them, and re-layouts: 92.4 us -> 13.4 us
  between operations: 26 us -> 1.32 us
    psum x9 -> x0, waiting for transfers between devices: 900 us -> none  [broadcast(): return lax.psum(jnp.where(mine, array, jnp.zeros_like(array)), axis)]
    another operation x68 -> x1, other arithmetic: 494 us -> 0.01 us  [tables(): table = jnp.stack([where, code]).astype(jnp.int32)]
    pallas_call x0 -> x2, Pallas kernels: none -> 402 us  [the longest x1 400 us: fused(): pl.pallas_call(kernel, out_shape=[jax.ShapeDtypeStruct((B, NP * B), F32),...]
    all_to_all x2 -> x0, waiting for transfers between devices: 229 us -> none  [the longest x1 229 us: body(): lax.all_to_all(outgoing, 'row', split_axis=0, concat_axis=0, tiled=True)]
    dot_general x7 -> x0, matrix products: 75.1 us -> none  [the longest x1 22.7 us: body(): summed = jnp.einsum('sq,sab->qab', positions, incoming, precision=precise)]
    another operation x52 -> x0, matrix products: 60.1 us -> none  [the longest x28 35.7 us: body(): lax.linalg.triangular_solve(factor, strip_now, left_side=False, lower=Tru...]
    another operation x73 -> x0, local copies, waits for them, and re-layouts: 40.5 us -> none  [the longest x57 38.9 us: body(): lax.linalg.triangular_solve(factor, strip_now, left_side=False, lower=Tru...]
    select_n x14 -> x1, other arithmetic: 20.9 us -> 0.01 us  [tables(): code = jnp.where(hit.any(axis=0), code, 2)]
  transfers between devices with their start and end apart: 11 -> 0, of which waited for: 10 -> 0; matrix products, arithmetic and copies ran while one was open for 2% -> 0% of each run, Pallas kernels for 0% -> 0%
where the time goes in v2:
time: 419 us
  Pallas kernels  402 us (96%)
  local copies, waits for them, and re-layouts  13.4 us (3%)
    pallas_call x1, Pallas kernels, fused(): pl.pallas_call(kernel, out_shape=[jax.ShapeDtypeStruct((B, NP * B), F32),...  400 us
    unnamed x8, local copies, waits for them, and re-layouts  12.8 us

profile of v2, /device:TPU:109, one launch (start us, length us, event | category | flops | bytes accessed | tf_op | source)
XLA Modules:
  0.0 418.6 jit_solution(1148655497090235193)
XLA Ops:
  1.3 0.7 iota_add_fusion
  2.0 0.8 fusion.4
  2.7 0.2 convert_reduce_fusion
  2.9 0.1 select_reduce_fusion.2.order
  3.0 0.1 select_reduce_fusion.1
  3.1 0.1 fusion.1
  3.2 0.6 pad.4.meta
  3.8 0.0 copy-start.1
  3.8 3.4 copy-done.1
  7.2 1.8 shard_map.59.child
  9.0 0.0 copy-start
  9.1 3.2 copy-done
  12.3 400.1 %shard_map.60 = (f32[512,2048]{1,0:T(8,128)}, f32[16,32,1024]{2,1,0:T(8,128)}) custom-call(f32[8,512,512]{2,1,0:T(8,128)} %copy-done, f32[16,32,1024]{2,1,0:T(8,128)} %bitcast.20, s32[8,128]{1,0:T(8,128)} %pad.4.meta), custom_call_target="tpu_custom_call" | custom-call | tf_op jit(solution)/shard_map/pallas_call | solution.py:723
  412.4 0.0 copy-start.2
  412.4 4.8 %copy.9 = f32[512,2048]{1,0:T(8,128)} copy(f32[512,2048]{1,0:T(8,128)} %get-tuple-element.13) | data formatting | bytes 8388608
  417.3 0.0 copy-done.2
  417.3 1.3 copy.10
  (3 shorter events, 0.0 us)
Async XLA Ops:
  3.8 3.4 copy-start.1
  9.0 3.2 copy-start
  412.4 4.9 %copy-start.2 = (f32[16,32,1024]{2,1,0:T(8,128)S(1)}, f32[16,32,1024]{2,1,0:T(8,128)}, u32[]{:S(2)}) copy-start(f32[16,32,1024]{2,1,0:T(8,128)} %get-tuple-element.5) | copy-start | bytes 6291460
